TPU v7x, 512 devices: a whole 4x4x16 slice. The times are simulated.
512 devices in a mesh: sect: 2 (over core), dp: 32 (over z_hi, y, x), tensor: 8 (over z_lo).
Axes of the slice: x: 4, y: 4, z: 16 (z_hi: 2, z_lo: 8; z = z_hi * 8 + z_lo), core: 2. Of those that a mesh axis runs over, the one named last changes fastest.
Arguments:
- teacher_rows: bfloat16 [1024, 16384], P('dp', ('sect', 'tensor')), may hold values from -48 to 48
- student_rows: bfloat16 [1024, 8192], P('dp', ('sect', 'tensor')), may hold values from -6 to 6
- projector: bfloat16 [8192, 16384], P(('sect', 'tensor'), 'dp'), may hold values from -0.0625 to 0.0625
- teacher_gain: float32 [16384], replicated, may hold values from 0.1 to 1.9
- student_gain: float32 [8192], replicated, may hold values from 0.1 to 1.9
Outputs:
- projector_grad: float32 [8192, 16384], P(('sect', 'tensor'), 'dp')
- input_grad: float32 [1024, 8192], P('dp', ('sect', 'tensor'))
All inputs are finite; a program needn't handle non-finite values.
Results may differ from a plain program's by a relative error of at most 0.0048.
Values may be sent and summed in bfloat16 or wider, within the bound.
A program may use at most 64 MiB of HBM per device.

v0:
```python
import math

import jax
import jax.numpy as jnp
from jax import lax
from jax.sharding import PartitionSpec as P

epsilon = 1e-05


def body(teacher_rows, student_rows, projector, teacher_gain, student_gain):
    st_count = lax.axis_size(("sect", "tensor"))
    dp_count = lax.axis_size("dp")
    st_index = lax.axis_index(("sect", "tensor"))
    dp_index = lax.axis_index("dp")
    tok_dev = student_rows.shape[0]
    per_piece = tok_dev // st_count
    width_t = teacher_rows.shape[1]
    width_s = student_rows.shape[1]
    teacher_f32 = teacher_rows.astype(jnp.float32)
    squares_sum = lax.psum(jnp.sum(teacher_f32 * teacher_f32, axis=-1), ("sect", "tensor"))
    inv_teacher = lax.rsqrt(squares_sum / (width_t * st_count) + epsilon)
    gain_cols = lax.dynamic_slice_in_dim(teacher_gain, st_index * width_t, width_t)
    normed = (teacher_f32 * inv_teacher[:, None] * gain_cols).astype(jnp.bfloat16)
    target = lax.all_to_all(
        lax.all_to_all(normed, ("sect", "tensor"), split_axis=0, concat_axis=1, tiled=True),
        "dp",
        split_axis=1,
        concat_axis=0,
        tiled=True,
    )
    student_f32 = student_rows.astype(jnp.float32)
    gain_rows = lax.dynamic_slice_in_dim(student_gain, st_index * width_s, width_s)
    raw_rows = lax.all_gather(student_rows, "dp", axis=0, tiled=True)
    raw_f32 = raw_rows.astype(jnp.float32)
    squares_all = lax.psum(jnp.sum(raw_f32 * raw_f32, axis=-1), ("sect", "tensor"))
    every_scale = lax.rsqrt(squares_all / (width_s * st_count) + epsilon)
    gathered = (raw_f32 * every_scale[:, None] * gain_rows).astype(jnp.bfloat16)
    own_scale = lax.dynamic_slice_in_dim(every_scale, dp_index * tok_dev, tok_dev)
    ordered = (
        gathered.reshape(dp_count, st_count, per_piece, width_s)
        .transpose(1, 0, 2, 3)
        .reshape(-1, width_s)
    )
    total_rows = ordered.shape[0]
    partial_all = jnp.dot(ordered, projector, preferred_element_type=jnp.float32)
    prediction_all = lax.psum(partial_all, ("sect", "tensor"))
    targets_all = lax.all_gather(target, ("sect", "tensor"), axis=0, tiled=True)
    residual_all = prediction_all - targets_all.astype(jnp.float32)
    errors_all = residual_all.astype(jnp.bfloat16)
    projector_grad = lax.dot_general(
        ordered, errors_all, (((0,), (0,)), ((), ())), preferred_element_type=jnp.float32
    ) / math.sqrt(total_rows)
    natural = (
        errors_all.reshape(st_count, dp_count, per_piece, -1)
        .transpose(1, 0, 2, 3)
        .reshape(total_rows, -1)
    )
    feature_grad = lax.psum_scatter(
        lax.dot_general(
            natural, projector, (((1,), (1,)), ((), ())), preferred_element_type=jnp.float32
        ),
        "dp",
        scatter_dimension=0,
        tiled=True,
    )
    unit_rows = student_f32 * own_scale[:, None]
    upstream = feature_grad * gain_rows
    inner_sum = lax.psum(jnp.sum(upstream * unit_rows, axis=-1), ("sect", "tensor"))
    inner_mean = inner_sum / (width_s * st_count)
    input_grad = own_scale[:, None] * (upstream - unit_rows * inner_mean[:, None])
    return (projector_grad, input_grad)


def solution(mesh):
    return jax.shard_map(
        body,
        mesh=mesh,
        in_specs=(
            P("dp", ("sect", "tensor")),
            P("dp", ("sect", "tensor")),
            P(("sect", "tensor"), "dp"),
            P(),
            P(),
        ),
        out_specs=(P(("sect", "tensor"), "dp"), P("dp", ("sect", "tensor"))),
        check_vma=False,
    )
```

profile of v0, /device:TPU:1, one launch (start us, length us, event | category | flops | bytes accessed | tf_op | source)
XLA Modules:
  0.0 879.8 jit_solution(14915638427327824890)
XLA Ops:
  7.2 0.7 all-gather.3.cloned.1.call-update
  8.0 0.8 dynamic_slice.9
  8.7 1.0 fusion.3
  9.7 118.2 %all-gather.3.cloned.1.call-done = bf16[1024,512]{1,0:T(8,128)(2,1)} async-done(((bf16[32,512]{1,0:T(8,128)(2,1)}), bf16[1024,512]{1,0:T(8,128)(2,1)}) %all-gather.3.cloned.1.call-update) | async-done | bytes 1048592 | tf_op jit(solution)/shard_map/all_gather | solution.py:34
  127.9 1.5 fusion
  129.4 47.3 %all-reduce = (f32[1024]{0:T(1024)S(1)}, f32[32]{0:T(128)S(1)}) all-reduce(f32[1024]{0:T(1024)S(1)} %fusion, f32[32]{0:T(128)S(1)} %fusion.3), channel_id=1, replica_groups=mesh['sect'=2,'dp'=32,'tensor'=8] {'sect','tensor'}, use_global_device_ids=true, to_apply=%region_1.0 | all-reduce | flops 1056 | bytes 8448 | tf_op jit(solution)/shard_map/psum | solution.py:36
  176.7 1.5 fusion.2
  178.2 0.4 reshape.29
  178.7 2.0 copy.12
  180.6 1.5 reshape.30
  182.1 2.0 fusion.6
  184.2 0.0 all-gather.5.cloned.1.call-start
  184.2 0.7 dynamic_slice.10
  184.9 0.1 fusion.5
  185.1 14.7 %all_to_all.35 = bf16[16,2,1024]{2,1,0:T(2,128)(2,1)S(1)} all-to-all(bf16[16,2,1024]{2,1,0:T(2,128)(2,1)S(1)} %all_to_all.26), channel_id=1, replica_groups=mesh['sect'=2,'dp'=32,'tensor'=8] {'sect','tensor'}, dimensions={0} | all-to-all | bytes 131072 | tf_op jit(solution)/shard_map/all_to_all | solution.py:26
  199.8 22.8 %all_to_all.36 = bf16[2,32,512]{2,0,1:T(2,128)(2,1)S(1)} all-to-all(bf16[2,32,512]{2,0,1:T(2,128)(2,1)S(1)} %bitcast.18), channel_id=1, replica_groups=mesh['sect'=2,'dp'=32,'tensor'=8] {'dp'}, dimensions={1} | all-to-all | bytes 131072 | tf_op jit(solution)/shard_map/all_to_all | solution.py:25
  222.6 0.7 all_to_all.32
  223.3 0.0 reduce-scatter.2.cloned.1.call-start
  223.3 174.0 %all-reduce.3.cloned.1.call-done = f32[1024,512]{1,0:T(8,128)} async-done(((f32[1024,512]{1,0:T(8,128)}), f32[1024,512]{1,0:T(8,128)}) %all-reduce.3.cloned.1.call-update) | async-done | bytes 2097168 | tf_op jit(solution)/shard_map/psum | solution.py:47
  397.4 104.3 %all-gather.5.cloned.1.call-done = bf16[1024,512]{1,0:T(8,128)(2,1)} async-done(((bf16[64,512]{1,0:T(8,128)(2,1)}), bf16[1024,512]{1,0:T(8,128)(2,1)}) %all-gather.5.cloned.1.call-update) | async-done | bytes 1048592 | tf_op jit(solution)/shard_map/all_gather | solution.py:48
  501.7 3.2 subtract_convert_fusion
  504.9 1.5 reshape.31
  506.3 2.1 copy.11
  508.4 1.5 reshape.32
  509.9 2.1 fusion.7
  512.0 0.1 dynamic_slice.11
  512.1 1.1 copy-done.1
  513.2 1.7 convolution_multiply_fusion
  514.9 288.7 %reduce-scatter.2.cloned.1.call-done = f32[32,512]{1,0:T(8,128)} async-done(((f32[1024,512]{1,0:T(8,128)}), f32[32,512]{1,0:T(8,128)}) %reduce-scatter.2.cloned.1.call-update) | async-done | bytes 65552 | tf_op jit(solution)/shard_map/reduce_scatter | solution.py:59
  803.6 1.0 multiply_reduce_fusion
  804.6 67.1 %psum.31 = f32[32]{0:T(128)S(1)} all-reduce(f32[32]{0:T(128)S(1)} %multiply_reduce_fusion), channel_id=1, replica_groups=mesh['sect'=2,'dp'=32,'tensor'=8] {'sect','tensor'}, use_global_device_ids=true, to_apply=%region_7.0 | all-reduce | flops 32 | bytes 256 | tf_op jit(solution)/shard_map/psum | solution.py:69
  871.7 1.5 subtract_multiply_fusion
  (16 shorter events, 0.2 us)
Async XLA Ops:
  7.2 175.0 %copy-start = (bf16[512,512]{1,0:T(8,128)(2,1)S(1)}, bf16[512,512]{1,0:T(8,128)(2,1)}, u32[]{:S(2)}) copy-start(bf16[512,512]{1,0:T(8,128)(2,1)} %param.7) | copy-start | bytes 1572868
  7.2 120.7 %all-gather.3.cloned.1.call-start = ((), (), s32[]{:S(2)}) async-start(), calls=%async_computation.3 | async-start | bytes 1081344 | tf_op jit(solution)/shard_map/all_gather | solution.py:34
  7.9 389.4 %all-reduce.3.cloned.1.call-start = ((), (), s32[]{:S(2)}) async-start(), calls=%async_computation.4 | async-start | bytes 4194304 | tf_op jit(solution)/shard_map/psum | solution.py:47
  182.1 2.8 copy-start.3
  184.2 317.5 %all-gather.5.cloned.1.call-start = ((), (), s32[]{:S(2)}) async-start(), calls=%async_computation.5 | async-start | bytes 1114112 | tf_op jit(solution)/shard_map/all_gather | solution.py:48
  223.3 580.3 %reduce-scatter.2.cloned.1.call-start = ((), (), s32[]{:S(2)}) async-start(), calls=%async_computation.6 | async-start | bytes 2162688 | tf_op jit(solution)/shard_map/reduce_scatter | solution.py:59
  512.0 1.2 copy-start.1
  513.2 290.4 %copy-start.2 = (bf16[32,512]{1,0:T(8,128)(2,1)S(1)}, bf16[32,512]{1,0:T(8,128)(2,1)}, u32[]{:S(2)}) copy-start(bf16[32,512]{1,0:T(8,128)(2,1)} %param.6) | copy-start | bytes 98308
Sparse Core Ops, SparseCore 0:
  12.3 115.5 all-gather.2
  184.3 213.0 all-reduce.2
  400.0 101.6 all-gather.4
  512.2 291.3 reduce-scatter.1
where the time goes:
time: 881 us; the launch traced here: 880 us
  waiting for transfers between devices  686 us (78%)
  blocking collectives  152 us (17%)
  between operations  13.9 us (2%)
  local copies, waits for them, and re-layouts  12.3 us (1%)
  other arithmetic  9.82 us (1%)
    reduce_scatter x1, waiting for transfers between devices, body(): lax.psum_scatter(lax.dot_general(natural, projector, (((1,), (1,)), ((),...  289 us
    psum x1, waiting for transfers between devices, body(): prediction_all = lax.psum(partial_all, ('sect', 'tensor'))  174 us
    all_gather x1, waiting for transfers between devices, body(): raw_rows = lax.all_gather(student_rows, 'dp', axis=0, tiled=True)  118 us
    all_gather x1, waiting for transfers between devices, body(): targets_all = lax.all_gather(target, ('sect', 'tensor'), axis=0, tiled=True)  104 us
    psum x1, blocking collectives, body(): lax.psum(jnp.sum(upstream * unit_rows, axis=-1), ('sect', 'tensor'))  67.1 us
    psum x1, blocking collectives, body(): lax.psum(jnp.sum(raw_f32 * raw_f32, axis=-1), ('sect', 'tensor'))  47.3 us
    all_to_all x1, blocking collectives, body(): lax.all_to_all(lax.all_to_all(normed, ('sect', 'tensor'), split_axis=0, c...  22.8 us
  transfers between devices with their start and end apart: 4, of which 4 were waited for; matrix products, arithmetic and copies ran while one was open for 0% of the time, Pallas kernels for 0%

commit v1 on v0

v1 whole, which is shorter than its diff:
```python
import math

import jax
import jax.numpy as jnp
from jax import lax
from jax.experimental import pallas as pl
from jax.experimental.pallas import tpu as pltpu
from jax.sharding import PartitionSpec as P

epsilon = 1e-05

MESH = pl.DeviceIdType.MESH
DT = 16384
DS = 8192
TOKENS = 1024
SECT = 2
NX = 4
NY = 4
NZH = 2
DP = NZH * NY * NX
QUADS = 2
INQ = 4
TENSOR = QUADS * INQ
ST = SECT * TENSOR
TOK = TOKENS // DP
WT = DT // ST
WS = DS // ST
WC = DT // DP
HC = WC // SECT
CHUNK = TENSOR * TOK
LANES = 128
SEMS = 120
F32 = jnp.float32
BF16 = jnp.bfloat16

N1, F1, F2, N2 = range(4)
NEAR = (N1, N2)


def kernel(
    teacher_hbm, student_hbm, proj_hbm, tgain_hbm, sgain_hbm,
    pgrad, igrad,
    teacher, student, proj, tgain, sgain,
    stat, stat2, total_send, total_far, raw_far, feats, tsend, trecv, part, yrecv, ssend, r1, acc, a_send, r2,
    errs, gnear, gfar, g1, hnear, hsend, hfar, g2near, g2last, g2far, zsend, zrecv,
    load_sems, send_sems, recv_sems,
):
    c = lax.axis_index("sect")
    d = lax.axis_index("dp")
    t = lax.axis_index("tensor")
    h, y, x = d // (NY * NX), (d // NX) % NY, d % NX
    qd, zi = t // INQ, t % INQ
    pa, pb = 1 - zi // 2, zi % 2
    st = c * TENSOR + t
    far = 1 - h
    yp, yb, xp, xb = y // 2, y % 2, x // 2, x % 2

    used = [0]
    sent = []

    def tickets(count):
        used[0] += count
        return range(used[0] - count, used[0])

    def dev(sect=None, dp=None, tensor=None):
        return {
            "sect": c if sect is None else sect,
            "dp": d if dp is None else dp,
            "tensor": t if tensor is None else tensor,
        }

    def send(i, src, dst, to, recv=None):
        op = pltpu.make_async_remote_copy(
            src_ref=src, dst_ref=dst, send_sem=send_sems.at[i],
            recv_sem=recv_sems.at[i if recv is None else recv],
            device_id=to, device_id_type=MESH,
        )
        op.start()
        sent.append(op)

    def arrived(i, dst, to):
        pltpu.make_async_remote_copy(
            src_ref=dst, dst_ref=dst, send_sem=send_sems.at[i], recv_sem=recv_sems.at[i],
            device_id=to, device_id_type=MESH,
        ).wait_recv()

    def at(zh, yy, xx):
        return dev(dp=zh * (NY * NX) + yy * NX + xx)

    def x_plus(k):
        return (x + k) % NX

    def y_plus(k):
        return (y + k) % NY

    y_mate, x_mate = y + 1 - 2 * yb, x + 1 - 2 * xb
    z_mate = at(far, y, x)
    sibling = dev(sect=1 - c)
    across = dev(tensor=(1 - qd) * INQ + zi)

    def in_quad(k):
        return dev(tensor=qd * INQ + (zi + k) % INQ)

    def place(k):
        other = (zi + k) % INQ
        return 1 - other // 2, other % 2

    def st_dev(k):
        other = (st + k) % ST
        return other, dev(sect=other // TENSOR, tensor=other % TENSOR)

    loads = [
        pltpu.make_async_copy(src, dst, load_sems.at[i])
        for i, (src, dst) in enumerate(
            ((student_hbm, student), (teacher_hbm, teacher), (sgain_hbm, sgain), (tgain_hbm, tgain), (proj_hbm, proj))
        )
    ]
    for op in loads:
        op.start()

    barrier = pltpu.get_barrier_semaphore()

    def hello(to):
        pl.semaphore_signal(barrier, inc=1, device_id=to, device_id_type=MESH)

    for k in range(1, ST):
        hello(st_dev(k)[1])
    for k in range(1, NY * NX):
        hello(at(h, y_plus(k // NX), x_plus(k % NX)))
    hello(z_mate)
    source = dict(sect=(d // 2) // TENSOR, tensor=(d // 2) % TENSOR)
    for zh, yy, xx in (
        (h, 2 * yp + pa, 2 * qd + pb),
        (far, 2 * pa + qd, 2 * xp + pb),
        (far, 2 * pa + qd, 2 * (1 - xp) + pb),
        (h, 2 * (1 - yp) + pa, 2 * qd + pb),
    ):
        hello(dev(dp=zh * (NY * NX) + yy * NX + xx, **source))

    rows = lax.broadcasted_iota(jnp.int32, (TOK, LANES), 0)
    lanes = lax.broadcasted_iota(jnp.int32, (TOK, LANES), 1)
    zero = jnp.zeros((TOK, LANES), F32)

    def column(row, first):
        return jnp.sum(jnp.where(lanes == rows + first, row, zero), axis=1, keepdims=True)

    loads[0].wait()
    sf = student[...].astype(F32)
    ssum = jnp.sum(sf * sf, axis=1, keepdims=True)
    loads[1].wait()
    tf = teacher[...].astype(F32)
    tsum = jnp.sum(tf * tf, axis=1, keepdims=True)
    spread = jnp.where(lanes == rows, tsum, zero) + jnp.where(lanes == rows + TOK, ssum, zero)
    stat[st] = jnp.sum(spread, axis=0, keepdims=True)

    pl.semaphore_wait(barrier, (ST - 1) + (NY * NX - 1) + 1 + 4)

    def exchange(ref):
        own = tickets(ST - 1)
        for k in range(1, ST):
            send(own[k - 1], ref.at[st], ref.at[st], st_dev(k)[1])

        def finish():
            for k in range(1, ST):
                other, where = st_dev(ST - k)
                arrived(own[k - 1], ref.at[other], where)
            return jnp.sum(ref[...], axis=0)

        return finish

    finish_stat = exchange(stat)
    raw_t, total_t = tickets(2)
    send(raw_t, student, raw_far, z_mate)

    loads[2].wait()
    sg = sgain[st]
    sg_row = jnp.concatenate([sg[k : k + 1, :] for k in range(WS // LANES)], axis=1)
    loads[3].wait()
    tg = tgain[st]

    total = finish_stat()
    inv_s = lax.rsqrt(column(total, TOK) / DS + epsilon)
    unit = sf * inv_s
    feats[h, y, x] = (unit * sg_row).astype(BF16)
    nx_t, nm_t = tickets(NX - 1), tickets(NX)
    for k in range(1, NX):
        send(nx_t[k - 1], feats.at[h, y, x], feats.at[h, y, x], at(h, y, x_plus(k)))
    for k in range(NX):
        send(nm_t[k], feats.at[h, y, x], feats.at[h, y, x], at(h, y_mate, x_plus(k)))
    total_send[...] = total
    send(total_t, total_send, total_far, z_mate)

    inv_t = lax.rsqrt(column(total, 0) / DT + epsilon)
    for k in range(WT // LANES):
        col = k * LANES
        value = tf[:, col : col + LANES] * inv_t * tg[k : k + 1, :]
        tsend[col // WC, (col % WC) // HC, :, col % HC : col % HC + LANES] = value.astype(BF16)

    ny_t = tickets(2)
    tt = tickets(4)
    ts = tickets(4)
    near_there = h == c
    to_a = jnp.where(near_there, yb, yp)
    to_q = jnp.where(near_there, xp, yb)
    for j in range(2):
        xp_there = ((2 * t + j) % NX) // 2
        yp_there = t // INQ
        slot = jnp.where(
            near_there,
            jnp.where(yp == yp_there, N1, N2),
            jnp.where(xp == xp_there, F1, F2),
        )
        for u in range(SECT):
            send(
                ts[2 * j + u], tsend.at[j, u], trecv.at[slot],
                dev(sect=u, dp=2 * st + j, tensor=to_q * INQ + (1 - to_a) * 2 + xb),
                tt[0] + slot,
            )

    arrived(raw_t, raw_far, z_mate)
    arrived(total_t, total_far, z_mate)
    inv_far = lax.rsqrt(column(total_far[...], TOK) / DS + epsilon)
    feats[far, y, x] = (raw_far[...].astype(F32) * inv_far * sg_row).astype(BF16)
    fy_t = tickets(NY - 1)
    for k in range(1, NY):
        send(fy_t[k - 1], feats.at[far, y, x], feats.at[far, y, x], at(h, y_plus(k), x))

    fx_t = tickets(3)

    def rows_of(ci):
        if ci in NEAR:
            return feats[h, pl.ds(2 * (yp if ci == N1 else 1 - yp), 2)].reshape(CHUNK, WS)
        return feats[far, :, pl.ds(2 * (xp if ci == F1 else 1 - xp), 2)].reshape(CHUNK, WS)

    def features_ready(ci):
        if ci == N1:
            for k in range(1, NX):
                xx = x_plus(NX - k)
                arrived(nx_t[k - 1], feats.at[h, y, xx], at(h, y, xx))
            for r in range(2):
                send(ny_t[r], feats.at[h, y], feats.at[h, y], at(h, 2 * (1 - yp) + r, x), ny_t[0] + yb)
            for k in range(NX):
                xx = x_plus(NX - k)
                arrived(nm_t[k], feats.at[h, y_mate, xx], at(h, y_mate, xx))
        elif ci == N2:
            for r in range(2):
                arrived(ny_t[r], feats.at[h, 2 * (1 - yp) + r], at(h, 2 * (1 - yp) + r, x))
        elif ci == F1:
            arrived(fx_t[0], feats.at[far, :, x_mate], at(h, y, x_mate))
            for r in range(2):
                send(
                    fx_t[1 + r], feats.at[far, :, x], feats.at[far, :, x], at(h, y, 2 * (1 - xp) + r), fx_t[1] + xb
                )
        else:
            for r in range(2):
                arrived(fx_t[1 + r], feats.at[far, :, 2 * (1 - xp) + r], at(h, y, 2 * (1 - xp) + r))

    def far_columns():
        for k in range(1, NY):
            yy = y_plus(NY - k)
            arrived(fy_t[k - 1], feats.at[far, yy, x], at(h, yy, x))
        send(fx_t[0], feats.at[far, :, x], feats.at[far, :, x], at(h, y, x_mate))

    pair_t, r1_t, r2_t = tickets(4), [tickets(INQ - 1) for _ in range(4)], tickets(4)
    e2_t, es_t = [tickets(INQ - 1) for _ in range(4)], tickets(4)
    g1_t = [tickets(3) for _ in range(3)]
    n2_t, f2_t, last_t = tickets(1), tickets(3), tickets(2 * NX)
    (z_t,) = tickets(1)

    def predict(ci):
        features_ready(ci)
        value = rows_of(ci)
        for u in range(SECT):
            half = jnp.dot(value, proj[:, u * HC : (u + 1) * HC], preferred_element_type=F32)
            part[ci, u] = half.reshape(2, 2, 2, TOK, HC)
        send(pair_t[ci], part.at[ci, 1 - c], yrecv.at[ci], sibling)

    def sum_pair(ci):
        arrived(pair_t[ci], yrecv.at[ci], sibling)
        value = part[ci, c] + yrecv[ci]
        part[ci, c] = value
        ssend[ci] = value.astype(BF16)
        for k in range(1, INQ):
            a, b = place(k)
            send(r1_t[ci][k - 1], ssend.at[ci, a, :, b], r1.at[ci, k - 1], in_quad(k))

    def sum_quad(ci):
        for k in range(1, INQ):
            arrived(r1_t[ci][k - 1], r1.at[ci, k - 1], in_quad(INQ - k))
        value = part[ci, c, pa, :, pb]
        for k in range(INQ - 1):
            value = value + r1[ci, k].astype(F32)
        acc[ci] = value
        arrived(tt[ci], trecv.at[ci], sibling)
        acc[ci, qd] = acc[ci, qd] - trecv[ci].astype(F32)
        a_send[ci] = acc[ci].astype(BF16)
        send(r2_t[ci], a_send.at[ci], r2.at[ci], across)

    def residual(ci):
        arrived(r2_t[ci], r2.at[ci], across)
        errs[ci, c, pa, :, pb] = (acc[ci] + r2[ci].astype(F32)).astype(BF16)
        for k in range(1, INQ):
            send(e2_t[ci][k - 1], errs.at[ci, c, pa, :, pb], errs.at[ci, c, pa, :, pb], in_quad(k))

    def errors_pair(ci):
        for k in range(1, INQ):
            a, b = place(INQ - k)
            arrived(e2_t[ci][k - 1], errs.at[ci, c, a, :, b], in_quad(INQ - k))
        send(es_t[ci], errs.at[ci, c], errs.at[ci, c], sibling)

    def back(ci):
        arrived(es_t[ci], errs.at[ci, 1 - c], sibling)
        value = None
        for u in range(SECT):
            term = lax.dot_general(
                errs[ci, u].reshape(CHUNK, HC), proj[:, u * HC : (u + 1) * HC], (((1,), (1,)), ((), ())),
                preferred_element_type=F32,
            )
            value = term if value is None else value + term
        value = value.astype(BF16)
        if ci in NEAR:
            gnear[NEAR.index(ci)] = value.reshape(2, NX, TOK, WS)
            if ci == N2:
                for r in range(2):
                    for k in range(NX):
                        xx = x_plus(k)
                        send(
                            last_t[NX * r + k], gnear.at[1, r, xx], g2last.at[NX * yb + k],
                            at(h, 2 * (1 - yp) + r, xx), last_t[0] + NX * yb + k,
                        )
                return
            for k in range(1, NX):
                xx = x_plus(k)
                send(g1_t[ci][k - 1], gnear.at[NEAR.index(ci), :, xx], g1.at[ci, k - 1], at(h, y, xx))
        else:
            gfar[ci - F1] = value.reshape(NY, 2, TOK, WS)
            for k in range(1, NY):
                yy = y_plus(k)
                send(g1_t[ci][k - 1], gfar.at[ci - F1, yy], g1.at[ci, k - 1], at(h, yy, x))

    def grad(ci):
        for u in range(SECT):
            term = lax.dot_general(
                rows_of(ci), errs[ci, u].reshape(CHUNK, HC), (((0,), (0,)), ((), ())), preferred_element_type=F32
            ) * (1.0 / math.sqrt(TOKENS))
            cols = slice(u * HC, (u + 1) * HC)
            pgrad[:, cols] = term if ci == N1 else pgrad[:, cols] + term

    def second(ci):
        for k in range(1, 4):
            where = at(h, y, x_plus(NX - k)) if ci in NEAR else at(h, y_plus(NY - k), x)
            arrived(g1_t[ci][k - 1], g1.at[ci, k - 1], where)
        value = gnear[NEAR.index(ci), :, x] if ci in NEAR else gfar[ci - F1, y]
        value = value.astype(F32)
        for k in range(3):
            value = value + g1[ci, k].astype(F32)
        if ci == N1:
            hnear[...] = value
            hsend[...] = value.astype(BF16)
            send(n2_t[0], hsend.at[1 - yb], g2near, at(h, y_mate, x))
        else:
            f = ci - F1
            hfar[f] = value
            if ci == F1:
                send(f2_t[0], hfar.at[f, 1 - xb], g2far.at[0], at(h, y, x_mate))
            else:
                for r in range(2):
                    send(f2_t[1 + r], hfar.at[f, r], g2far.at[1 + xb], at(h, y, 2 * (1 - xp) + r), f2_t[1] + xb)

    def send_far():
        arrived(f2_t[0], g2far.at[0], at(h, y, x_mate))
        for r in range(2):
            arrived(f2_t[1 + r], g2far.at[1 + r], at(h, y, 2 * (1 - xp) + r))
        zsend[...] = (hfar[0, xb] + g2far[0] + g2far[1] + g2far[2]).astype(BF16)
        send(z_t, zsend, zrecv, z_mate)

    loads[4].wait()
    predict(N1)
    far_columns()
    sum_pair(N1)
    sum_quad(N1)
    predict(F1)
    residual(N1)
    sum_pair(F1)
    predict(F2)
    sum_quad(F1)
    sum_pair(F2)
    errors_pair(N1)
    predict(N2)
    residual(F1)
    back(N1)
    sum_quad(F2)
    sum_pair(N2)
    grad(N1)
    errors_pair(F1)
    residual(F2)
    sum_quad(N2)
    back(F1)
    second(N1)
    grad(F1)
    errors_pair(F2)
    residual(N2)
    back(F2)
    second(F1)
    grad(F2)
    errors_pair(N2)
    second(F2)
    back(N2)
    send_far()
    grad(N2)

    for op in sent:
        op.wait_send()
    sent.clear()

    arrived(n2_t[0], g2near, at(h, y_mate, x))
    arrived(z_t, zrecv, z_mate)
    feature_grad = hnear[yb] + g2near[...].astype(F32) + zrecv[...].astype(F32)
    for r in range(2):
        for k in range(NX):
            slot = NX * r + k
            arrived(last_t[slot], g2last.at[slot], at(h, 2 * (1 - yp) + r, x_plus(NX - k)))
            feature_grad = feature_grad + g2last[slot].astype(F32)
    upstream = feature_grad * sg_row

    inner = jnp.sum(upstream * unit, axis=1, keepdims=True)
    stat2[st] = jnp.sum(jnp.where(lanes == rows, inner, zero), axis=0, keepdims=True)
    inner_mean = column(exchange(stat2)(), 0) / DS
    igrad[...] = inv_s * (upstream - unit * inner_mean)

    for op in sent:
        op.wait_send()
    assert used[0] <= SEMS, used


def body(teacher_rows, student_rows, projector, teacher_gain, student_gain):
    vmem = pl.BlockSpec(memory_space=pltpu.VMEM)
    piece = (2, 2, 2, TOK, HC)
    return pl.pallas_call(
        kernel,
        out_shape=(
            jax.ShapeDtypeStruct((WS, WC), F32),
            jax.ShapeDtypeStruct((TOK, WS), F32),
        ),
        in_specs=[pl.BlockSpec(memory_space=pltpu.HBM)] * 5,
        out_specs=(vmem, vmem),
        scratch_shapes=[
            pltpu.VMEM((TOK, WT), BF16),
            pltpu.VMEM((TOK, WS), BF16),
            pltpu.VMEM((WS, WC), BF16),
            pltpu.VMEM((ST, WT // LANES, LANES), F32),
            pltpu.VMEM((ST, WS // LANES, LANES), F32),
            pltpu.VMEM((ST, 1, LANES), F32),
            pltpu.VMEM((ST, 1, LANES), F32),
            pltpu.VMEM((1, LANES), F32),
            pltpu.VMEM((1, LANES), F32),
            pltpu.VMEM((TOK, WS), BF16),
            pltpu.VMEM((NZH, NY, NX, TOK, WS), BF16),
            pltpu.VMEM((2, SECT, TOK, HC), BF16),
            pltpu.VMEM((4, TOK, HC), BF16),
            pltpu.VMEM((4, SECT) + piece, F32),
            pltpu.VMEM((4,) + piece, F32),
            pltpu.VMEM((4,) + piece, BF16),
            pltpu.VMEM((4, INQ - 1, QUADS, TOK, HC), BF16),
            pltpu.VMEM((4, QUADS, TOK, HC), F32),
            pltpu.VMEM((4, QUADS, TOK, HC), BF16),
            pltpu.VMEM((4, QUADS, TOK, HC), BF16),
            pltpu.VMEM((4, SECT) + piece, BF16),
            pltpu.VMEM((2, 2, NX, TOK, WS), BF16),
            pltpu.VMEM((2, NY, 2, TOK, WS), BF16),
            pltpu.VMEM((3, 3, 2, TOK, WS), BF16),
            pltpu.VMEM((2, TOK, WS), F32),
            pltpu.VMEM((2, TOK, WS), BF16),
            pltpu.VMEM((2, 2, TOK, WS), F32),
            pltpu.VMEM((TOK, WS), BF16),
            pltpu.VMEM((2 * NX, TOK, WS), BF16),
            pltpu.VMEM((3, TOK, WS), F32),
            pltpu.VMEM((TOK, WS), BF16),
            pltpu.VMEM((TOK, WS), BF16),
            pltpu.SemaphoreType.DMA((5,)),
            pltpu.SemaphoreType.DMA((SEMS,)),
            pltpu.SemaphoreType.DMA((SEMS,)),
        ],
        compiler_params=pltpu.CompilerParams(
            collective_id=0, has_side_effects=True, vmem_limit_bytes=32 * 1024 * 1024
        ),
    )(
        teacher_rows,
        student_rows,
        projector,
        teacher_gain.reshape(ST, WT // LANES, LANES),
        student_gain.reshape(ST, WS // LANES, LANES),
    )


def solution(mesh):
    return jax.shard_map(
        body,
        mesh=mesh,
        in_specs=(
            P("dp", ("sect", "tensor")),
            P("dp", ("sect", "tensor")),
            P(("sect", "tensor"), "dp"),
            P(),
            P(),
        ),
        out_specs=(P(("sect", "tensor"), "dp"), P("dp", ("sect", "tensor"))),
        check_vma=False,
    )
```

time: 881 us -> 110 us (0.12)
  waiting for transfers between devices: 686 us -> 0 us
  blocking collectives: 152 us -> 0 us
  Pallas kernels: 0 us -> 104 us
  between operations: 13.9 us -> 0.65 us
  other arithmetic: 9.82 us -> 0 us
    reduce_scatter x1 -> x0, waiting for transfers between devices: 289 us -> none  [body(): lax.psum_scatter(lax.dot_general(natural, projector, (((1,), (1,)), ((),...]
    all_gather x2 -> x0, waiting for transfers between devices: 223 us -> none  [the longest x1 118 us: body(): raw_rows = lax.all_gather(student_rows, 'dp', axis=0, tiled=True)]
    psum x1 -> x0, waiting for transfers between devices: 174 us -> none  [body(): prediction_all = lax.psum(partial_all, ('sect', 'tensor'))]
    psum x2 -> x0, blocking collectives: 114 us -> none  [the longest x1 67.1 us: body(): lax.psum(jnp.sum(upstream * unit_rows, axis=-1), ('sect', 'tensor'))]
    pallas_call x0 -> x1, Pallas kernels: none -> 104 us  [body(): pl.pallas_call(kernel, out_shape=(jax.ShapeDtypeStruct((WS, WC), F32), ja...]
    all_to_all x2 -> x0, blocking collectives: 37.5 us -> none  [the longest x1 22.8 us: body(): lax.all_to_all(lax.all_to_all(normed, ('sect', 'tensor'), split_axis=0, c...]
    reshape x6 -> x0, local copies, waits for them, and re-layouts: 8.92 us -> none  [the longest x2 3.57 us: body(): errors_all.reshape(st_count, dp_count, per_piece, -1).transpose(1, 0, 2, 3)]
  transfers between devices with their start and end apart: 4 -> 0, of which waited for: 4 -> 0; matrix products, arithmetic and copies ran while one was open for 0% -> 0% of each run, Pallas kernels for 0% -> 0%
where the time goes in v1:
time: 110 us
  Pallas kernels  104 us (95%)
  local copies, waits for them, and re-layouts  5.83 us (5%)
    pallas_call x1, Pallas kernels, body(): pl.pallas_call(kernel, out_shape=(jax.ShapeDtypeStruct((WS, WC), F32), ja...  104 us
    unnamed x12, local copies, waits for them, and re-layouts  5.83 us

profile of v1, /device:TPU:1, one launch (start us, length us, event | category | flops | bytes accessed | tf_op | source)
XLA Modules:
  0.0 110.1 jit_solution(6595277888795059459)
XLA Ops:
  0.6 0.0 copy-start
  0.6 1.0 copy-done
  1.7 0.0 copy-start.1
  1.7 0.8 copy-done.1
  2.5 0.0 copy-start.2
  2.5 0.8 copy-done.2
  3.4 0.0 copy-start.3
  3.4 0.8 copy-done.3
  4.1 0.0 copy-start.4
  4.1 0.8 copy-done.4
  4.9 103.6 %shard_map.68 = (f32[512,512]{1,0:T(8,128)S(1)}, f32[32,512]{1,0:T(8,128)S(1)}) custom-call(bf16[32,1024]{1,0:T(8,128)(2,1)S(1)} %copy-done.1, bf16[32,512]{1,0:T(8,128)(2,1)S(1)} %copy-done.3, bf16[512,512]{1,0:T(8,128)(2,1)S(1)} %copy-done, f32[16,8,128]{2,1,0:T(8,128)S(1)} %bitcast.2, f32[16,4,128]{2,1,0:T(4,128)S(1)} %bitcast.3), custom_call_target="tpu_custom_call" | custom-call | tf_op jit(solution)/shard_map/pallas_call | solution.py:439
  108.5 1.0 copy.9
  109.5 0.6 copy.10
Async XLA Ops:
  0.6 1.0 copy-start
  1.7 0.8 copy-start.1
  2.5 0.8 copy-start.2
  3.4 0.8 copy-start.3
  4.1 0.8 copy-start.4

commit v2 on v1

--- a/solution.py
+++ b/solution.py
@@ -39,8 +39,8 @@
 
 def kernel(
     teacher_hbm, student_hbm, proj_hbm, tgain_hbm, sgain_hbm,
-    pgrad, igrad,
-    teacher, student, proj, tgain, sgain,
+    pgrad_hbm, igrad_hbm,
+    pgrad, igrad, pt, ft, teacher, student, proj, tgain, sgain,
     stat, stat2, total_send, total_far, raw_far, feats, tsend, trecv, part, yrecv, ssend, r1, acc, a_send, r2,
     errs, gnear, gfar, g1, hnear, hsend, hfar, g2near, g2last, g2far, zsend, zrecv,
     load_sems, send_sems, recv_sems,
@@ -178,6 +178,9 @@
     loads[3].wait()
     tg = tgain[st]
 
+    loads[4].wait()
+    pt[...] = proj[...].T
+
     total = finish_stat()
     inv_s = lax.rsqrt(column(total, TOK) / DS + epsilon)
     unit = sf * inv_s
@@ -199,6 +202,7 @@
     ny_t = tickets(2)
     tt = tickets(4)
     ts = tickets(4)
+    rows_out = []
     near_there = h == c
     to_a = jnp.where(near_there, yb, yp)
     to_q = jnp.where(near_there, xp, yb)
@@ -211,11 +215,24 @@
             jnp.where(xp == xp_there, F1, F2),
         )
         for u in range(SECT):
-            send(
-                ts[2 * j + u], tsend.at[j, u], trecv.at[slot],
-                dev(sect=u, dp=2 * st + j, tensor=to_q * INQ + (1 - to_a) * 2 + xb),
-                tt[0] + slot,
+            rows_out.append(
+                pltpu.make_async_remote_copy(
+                    src_ref=tsend.at[j, u], dst_ref=trecv.at[slot],
+                    send_sem=send_sems.at[ts[2 * j + u]], recv_sem=recv_sems.at[tt[0] + slot],
+                    device_id=dev(sect=u, dp=2 * st + j, tensor=to_q * INQ + (1 - to_a) * 2 + xb),
+                    device_id_type=MESH,
+                )
             )
+
+    first_chunk = jnp.logical_and(near_there, yp == t // INQ)
+
+    def send_teacher(now):
+        @pl.when(now)
+        def _():
+            for op in rows_out:
+                op.start()
+
+    send_teacher(first_chunk)
 
     arrived(raw_t, raw_far, z_mate)
     arrived(total_t, total_far, z_mate)
@@ -237,8 +254,6 @@
             for k in range(1, NX):
                 xx = x_plus(NX - k)
                 arrived(nx_t[k - 1], feats.at[h, y, xx], at(h, y, xx))
-            for r in range(2):
-                send(ny_t[r], feats.at[h, y], feats.at[h, y], at(h, 2 * (1 - yp) + r, x), ny_t[0] + yb)
             for k in range(NX):
                 xx = x_plus(NX - k)
                 arrived(nm_t[k], feats.at[h, y_mate, xx], at(h, y_mate, xx))
@@ -261,6 +276,10 @@
             arrived(fy_t[k - 1], feats.at[far, yy, x], at(h, yy, x))
         send(fx_t[0], feats.at[far, :, x], feats.at[far, :, x], at(h, y, x_mate))
 
+    def near_rows():
+        for r in range(2):
+            send(ny_t[r], feats.at[h, y], feats.at[h, y], at(h, 2 * (1 - yp) + r, x), ny_t[0] + yb)
+
     pair_t, r1_t, r2_t = tickets(4), [tickets(INQ - 1) for _ in range(4)], tickets(4)
     e2_t, es_t = [tickets(INQ - 1) for _ in range(4)], tickets(4)
     g1_t = [tickets(3) for _ in range(3)]
@@ -312,9 +331,8 @@
         arrived(es_t[ci], errs.at[ci, 1 - c], sibling)
         value = None
         for u in range(SECT):
-            term = lax.dot_general(
-                errs[ci, u].reshape(CHUNK, HC), proj[:, u * HC : (u + 1) * HC], (((1,), (1,)), ((), ())),
-                preferred_element_type=F32,
+            term = jnp.dot(
+                errs[ci, u].reshape(CHUNK, HC), pt[u * HC : (u + 1) * HC, :], preferred_element_type=F32
             )
             value = term if value is None else value + term
         value = value.astype(BF16)
@@ -338,11 +356,12 @@
                 yy = y_plus(k)
                 send(g1_t[ci][k - 1], gfar.at[ci - F1, yy], g1.at[ci, k - 1], at(h, yy, x))
 
+    def turn(ci):
+        ft[ci] = rows_of(ci).T
+
     def grad(ci):
         for u in range(SECT):
-            term = lax.dot_general(
-                rows_of(ci), errs[ci, u].reshape(CHUNK, HC), (((0,), (0,)), ((), ())), preferred_element_type=F32
-            ) * (1.0 / math.sqrt(TOKENS))
+            term = jnp.dot(ft[ci], errs[ci, u].reshape(CHUNK, HC), preferred_element_type=F32)
             cols = slice(u * HC, (u + 1) * HC)
             pgrad[:, cols] = term if ci == N1 else pgrad[:, cols] + term
 
@@ -374,23 +393,31 @@
         zsend[...] = (hfar[0, xb] + g2far[0] + g2far[1] + g2far[2]).astype(BF16)
         send(z_t, zsend, zrecv, z_mate)
 
-    loads[4].wait()
+    store_pgrad = pltpu.make_async_copy(pgrad, pgrad_hbm, load_sems.at[5])
+    store_igrad = pltpu.make_async_copy(igrad, igrad_hbm, load_sems.at[6])
+
     predict(N1)
     far_columns()
     sum_pair(N1)
+    send_teacher(jnp.logical_not(first_chunk))
+    turn(N1)
+    predict(F1)
+    near_rows()
     sum_quad(N1)
-    predict(F1)
+    sum_pair(F1)
+    turn(F1)
     residual(N1)
-    sum_pair(F1)
     predict(F2)
     sum_quad(F1)
     sum_pair(F2)
+    turn(F2)
     errors_pair(N1)
     predict(N2)
     residual(F1)
     back(N1)
     sum_quad(F2)
     sum_pair(N2)
+    turn(N2)
     grad(N1)
     errors_pair(F1)
     residual(F2)
@@ -408,6 +435,8 @@
     back(N2)
     send_far()
     grad(N2)
+    store_pgrad.start()
+    sent.extend(rows_out)
 
     for op in sent:
         op.wait_send()
@@ -427,24 +456,31 @@
     stat2[st] = jnp.sum(jnp.where(lanes == rows, inner, zero), axis=0, keepdims=True)
     inner_mean = column(exchange(stat2)(), 0) / DS
     igrad[...] = inv_s * (upstream - unit * inner_mean)
+    store_igrad.start()
 
     for op in sent:
         op.wait_send()
+    store_pgrad.wait()
+    store_igrad.wait()
     assert used[0] <= SEMS, used
 
 
 def body(teacher_rows, student_rows, projector, teacher_gain, student_gain):
-    vmem = pl.BlockSpec(memory_space=pltpu.VMEM)
+    anywhere = pl.BlockSpec(memory_space=pl.ANY)
     piece = (2, 2, 2, TOK, HC)
-    return pl.pallas_call(
+    summed, input_grad = pl.pallas_call(
         kernel,
         out_shape=(
             jax.ShapeDtypeStruct((WS, WC), F32),
             jax.ShapeDtypeStruct((TOK, WS), F32),
         ),
-        in_specs=[pl.BlockSpec(memory_space=pltpu.HBM)] * 5,
-        out_specs=(vmem, vmem),
+        in_specs=[anywhere] * 5,
+        out_specs=(anywhere, anywhere),
         scratch_shapes=[
+            pltpu.VMEM((WS, WC), F32),
+            pltpu.VMEM((TOK, WS), F32),
+            pltpu.VMEM((WC, WS), BF16),
+            pltpu.VMEM((4, WS, CHUNK), BF16),
             pltpu.VMEM((TOK, WT), BF16),
             pltpu.VMEM((TOK, WS), BF16),
             pltpu.VMEM((WS, WC), BF16),
@@ -477,12 +513,12 @@
             pltpu.VMEM((3, TOK, WS), F32),
             pltpu.VMEM((TOK, WS), BF16),
             pltpu.VMEM((TOK, WS), BF16),
-            pltpu.SemaphoreType.DMA((5,)),
+            pltpu.SemaphoreType.DMA((7,)),
             pltpu.SemaphoreType.DMA((SEMS,)),
             pltpu.SemaphoreType.DMA((SEMS,)),
         ],
         compiler_params=pltpu.CompilerParams(
-            collective_id=0, has_side_effects=True, vmem_limit_bytes=32 * 1024 * 1024
+            collective_id=0, has_side_effects=True, vmem_limit_bytes=56 * 1024 * 1024
         ),
     )(
         teacher_rows,
@@ -491,6 +527,7 @@
         teacher_gain.reshape(ST, WT // LANES, LANES),
         student_gain.reshape(ST, WS // LANES, LANES),
     )
+    return summed * (1.0 / math.sqrt(TOKENS)), input_grad
 
 
 def solution(mesh):

time: 110 us -> 106 us (0.964)
  the two profiles are of different devices: /device:TPU:1 before, /device:TPU:6 now
where the time goes in v2:
time: 106 us
  Pallas kernels  102 us (96%)
  other arithmetic  2.32 us (2%)
    pallas_call x1, Pallas kernels, body(): pl.pallas_call(kernel, out_shape=(jax.ShapeDtypeStruct((WS, WC), F32), ja...  102 us
    mul x1, other arithmetic, body(): return (summed * (1.0 / math.sqrt(TOKENS)), input_grad)  2.32 us

profile of v2, /device:TPU:6, one launch (start us, length us, event | category | flops | bytes accessed | tf_op | source)
XLA Modules:
  0.0 105.8 jit_solution(12763736462412964152)
XLA Ops:
  0.6 102.2 %shard_map.68 = (f32[512,512]{1,0:T(8,128)}, f32[32,512]{1,0:T(8,128)}) custom-call(bf16[32,1024]{1,0:T(8,128)(2,1)} %teacher_hbm.1, bf16[32,512]{1,0:T(8,128)(2,1)} %student_hbm.1, bf16[512,512]{1,0:T(8,128)(2,1)} %proj_hbm.1, f32[16,8,128]{2,1,0:T(8,128)} %bitcast.2, f32[16,4,128]{2,1,0:T(4,128)} %bitcast.3), custom_call_target="tpu_custom_call" | custom-call | tf_op jit(solution)/shard_map/pallas_call | solution.py:471
  102.8 0.0 copy-start
  102.9 2.3 %broadcast_multiply_fusion = f32[512,512]{1,0:T(8,128)} fusion(f32[512,512]{1,0:T(8,128)} %get-tuple-element.4), kind=kLoop, calls=%fused_computation | loop fusion | flops 262144 | bytes 2097152 | tf_op jit(solution)/shard_map/mul | solution.py:530
  105.2 0.0 copy-done
  105.2 0.6 copy.8
Async XLA Ops:
  102.8 2.3 %copy-start = (f32[32,512]{1,0:T(8,128)S(1)}, f32[32,512]{1,0:T(8,128)}, u32[]{:S(2)}) copy-start(f32[32,512]{1,0:T(8,128)} %get-tuple-element.9) | copy-start | bytes 196612

commit v3 on v2

--- a/solution.py
+++ b/solution.py
@@ -29,7 +29,7 @@
 HC = WC // SECT
 CHUNK = TENSOR * TOK
 LANES = 128
-SEMS = 120
+SEMS = 144
 F32 = jnp.float32
 BF16 = jnp.bfloat16
 
@@ -42,7 +42,7 @@
     pgrad_hbm, igrad_hbm,
     pgrad, igrad, pt, ft, teacher, student, proj, tgain, sgain,
     stat, stat2, total_send, total_far, raw_far, feats, tsend, trecv, part, yrecv, ssend, r1, acc, a_send, r2,
-    errs, gnear, gfar, g1, hnear, hsend, hfar, g2near, g2last, g2far, zsend, zrecv,
+    errs, gnear, gfar, gnear_in, gfar_in, zsend, zrecv,
     load_sems, send_sems, recv_sems,
 ):
     c = lax.axis_index("sect")
@@ -97,6 +97,23 @@
     z_mate = at(far, y, x)
     sibling = dev(sect=1 - c)
     across = dev(tensor=(1 - qd) * INQ + zi)
+
+    def peers(ci):
+        first, out = ci in (N1, F1), []
+        for r in range(2):
+            for k in range(4):
+                if first and r == 0 and k == 0:
+                    continue
+                if ci in NEAR:
+                    line = (y, y_mate)[r] if first else 2 * (1 - yp) + r
+                    to, of, mine = (line, x_plus(k)), (line, x_plus(NX - k)), yb
+                else:
+                    line = (x, x_mate)[r] if first else 2 * (1 - xp) + r
+                    to, of, mine = (y_plus(k), line), (y_plus(NY - k), line), xb
+                here = 4 * r + k - 1 if first else 7 + 4 * r + k
+                there = here if first else 7 + 4 * mine + k
+                out.append((to, of, there, here))
+        return out
 
     def in_quad(k):
         return dev(tensor=qd * INQ + (zi + k) % INQ)
@@ -185,13 +202,17 @@
     inv_s = lax.rsqrt(column(total, TOK) / DS + epsilon)
     unit = sf * inv_s
     feats[h, y, x] = (unit * sg_row).astype(BF16)
-    nx_t, nm_t = tickets(NX - 1), tickets(NX)
-    for k in range(1, NX):
-        send(nx_t[k - 1], feats.at[h, y, x], feats.at[h, y, x], at(h, y, x_plus(k)))
-    for k in range(NX):
-        send(nm_t[k], feats.at[h, y, x], feats.at[h, y, x], at(h, y_mate, x_plus(k)))
+    near_t, far_t = tickets(15), tickets(15)
+
+    def spread(ci):
+        zh, base = (h, near_t[0]) if ci in NEAR else (far, far_t[0])
+        for to, _, there, here in peers(ci):
+            send(base + here, feats.at[zh, y, x], feats.at[zh, y, x], at(h, *to), base + there)
+
+    spread(N1)
     total_send[...] = total
     send(total_t, total_send, total_far, z_mate)
+    spread(N2)
 
     inv_t = lax.rsqrt(column(total, 0) / DT + epsilon)
     for k in range(WT // LANES):
@@ -199,7 +220,6 @@
         value = tf[:, col : col + LANES] * inv_t * tg[k : k + 1, :]
         tsend[col // WC, (col % WC) // HC, :, col % HC : col % HC + LANES] = value.astype(BF16)
 
-    ny_t = tickets(2)
     tt = tickets(4)
     ts = tickets(4)
     rows_out = []
@@ -234,15 +254,13 @@
 
     send_teacher(first_chunk)
 
-    arrived(raw_t, raw_far, z_mate)
-    arrived(total_t, total_far, z_mate)
-    inv_far = lax.rsqrt(column(total_far[...], TOK) / DS + epsilon)
-    feats[far, y, x] = (raw_far[...].astype(F32) * inv_far * sg_row).astype(BF16)
-    fy_t = tickets(NY - 1)
-    for k in range(1, NY):
-        send(fy_t[k - 1], feats.at[far, y, x], feats.at[far, y, x], at(h, y_plus(k), x))
-
-    fx_t = tickets(3)
+    def far_in():
+        arrived(raw_t, raw_far, z_mate)
+        arrived(total_t, total_far, z_mate)
+        inv_far = lax.rsqrt(column(total_far[...], TOK) / DS + epsilon)
+        feats[far, y, x] = (raw_far[...].astype(F32) * inv_far * sg_row).astype(BF16)
+        spread(F1)
+        spread(F2)
 
     def rows_of(ci):
         if ci in NEAR:
@@ -250,40 +268,13 @@
         return feats[far, :, pl.ds(2 * (xp if ci == F1 else 1 - xp), 2)].reshape(CHUNK, WS)
 
     def features_ready(ci):
-        if ci == N1:
-            for k in range(1, NX):
-                xx = x_plus(NX - k)
-                arrived(nx_t[k - 1], feats.at[h, y, xx], at(h, y, xx))
-            for k in range(NX):
-                xx = x_plus(NX - k)
-                arrived(nm_t[k], feats.at[h, y_mate, xx], at(h, y_mate, xx))
-        elif ci == N2:
-            for r in range(2):
-                arrived(ny_t[r], feats.at[h, 2 * (1 - yp) + r], at(h, 2 * (1 - yp) + r, x))
-        elif ci == F1:
-            arrived(fx_t[0], feats.at[far, :, x_mate], at(h, y, x_mate))
-            for r in range(2):
-                send(
-                    fx_t[1 + r], feats.at[far, :, x], feats.at[far, :, x], at(h, y, 2 * (1 - xp) + r), fx_t[1] + xb
-                )
-        else:
-            for r in range(2):
-                arrived(fx_t[1 + r], feats.at[far, :, 2 * (1 - xp) + r], at(h, y, 2 * (1 - xp) + r))
-
-    def far_columns():
-        for k in range(1, NY):
-            yy = y_plus(NY - k)
-            arrived(fy_t[k - 1], feats.at[far, yy, x], at(h, yy, x))
-        send(fx_t[0], feats.at[far, :, x], feats.at[far, :, x], at(h, y, x_mate))
-
-    def near_rows():
-        for r in range(2):
-            send(ny_t[r], feats.at[h, y], feats.at[h, y], at(h, 2 * (1 - yp) + r, x), ny_t[0] + yb)
+        zh, base = (h, near_t[0]) if ci in NEAR else (far, far_t[0])
+        for _, of, _, here in peers(ci):
+            arrived(base + here, feats.at[zh, of[0], of[1]], at(h, *of))
 
     pair_t, r1_t, r2_t = tickets(4), [tickets(INQ - 1) for _ in range(4)], tickets(4)
     e2_t, es_t = [tickets(INQ - 1) for _ in range(4)], tickets(4)
-    g1_t = [tickets(3) for _ in range(3)]
-    n2_t, f2_t, last_t = tickets(1), tickets(3), tickets(2 * NX)
+    gnear_t, gfar_t = tickets(15), tickets(15)
     (z_t,) = tickets(1)
 
     def predict(ci):
@@ -336,104 +327,78 @@
             )
             value = term if value is None else value + term
         value = value.astype(BF16)
+        n = 0 if ci in (N1, F1) else 1
         if ci in NEAR:
-            gnear[NEAR.index(ci)] = value.reshape(2, NX, TOK, WS)
-            if ci == N2:
-                for r in range(2):
-                    for k in range(NX):
-                        xx = x_plus(k)
-                        send(
-                            last_t[NX * r + k], gnear.at[1, r, xx], g2last.at[NX * yb + k],
-                            at(h, 2 * (1 - yp) + r, xx), last_t[0] + NX * yb + k,
-                        )
-                return
-            for k in range(1, NX):
-                xx = x_plus(k)
-                send(g1_t[ci][k - 1], gnear.at[NEAR.index(ci), :, xx], g1.at[ci, k - 1], at(h, y, xx))
+            gnear[n] = value.reshape(2, NX, TOK, WS)
         else:
-            gfar[ci - F1] = value.reshape(NY, 2, TOK, WS)
-            for k in range(1, NY):
-                yy = y_plus(k)
-                send(g1_t[ci][k - 1], gfar.at[ci - F1, yy], g1.at[ci, k - 1], at(h, yy, x))
+            gfar[n] = value.reshape(NY, 2, TOK, WS)
+        for to, _, there, here in peers(ci):
+            if ci in NEAR:
+                send(gnear_t[here], gnear.at[n, to[0] % 2, to[1]], gnear_in.at[there], at(h, *to), gnear_t[0] + there)
+            else:
+                send(gfar_t[here], gfar.at[n, to[0], to[1] % 2], gfar_in.at[there], at(h, *to), gfar_t[0] + there)
+
+    def collect(value, slots, sems, chunks):
+        value = value.astype(F32)
+        for ci in chunks:
+            for _, of, _, here in peers(ci):
+                arrived(sems[here], slots.at[here], at(h, *of))
+                value = value + slots[here].astype(F32)
+        return value
 
     def turn(ci):
         ft[ci] = rows_of(ci).T
+
+    done = []
 
     def grad(ci):
         for u in range(SECT):
             term = jnp.dot(ft[ci], errs[ci, u].reshape(CHUNK, HC), preferred_element_type=F32)
             cols = slice(u * HC, (u + 1) * HC)
-            pgrad[:, cols] = term if ci == N1 else pgrad[:, cols] + term
-
-    def second(ci):
-        for k in range(1, 4):
-            where = at(h, y, x_plus(NX - k)) if ci in NEAR else at(h, y_plus(NY - k), x)
-            arrived(g1_t[ci][k - 1], g1.at[ci, k - 1], where)
-        value = gnear[NEAR.index(ci), :, x] if ci in NEAR else gfar[ci - F1, y]
-        value = value.astype(F32)
-        for k in range(3):
-            value = value + g1[ci, k].astype(F32)
-        if ci == N1:
-            hnear[...] = value
-            hsend[...] = value.astype(BF16)
-            send(n2_t[0], hsend.at[1 - yb], g2near, at(h, y_mate, x))
-        else:
-            f = ci - F1
-            hfar[f] = value
-            if ci == F1:
-                send(f2_t[0], hfar.at[f, 1 - xb], g2far.at[0], at(h, y, x_mate))
-            else:
-                for r in range(2):
-                    send(f2_t[1 + r], hfar.at[f, r], g2far.at[1 + xb], at(h, y, 2 * (1 - xp) + r), f2_t[1] + xb)
+            pgrad[:, cols] = term if not done else pgrad[:, cols] + term
+        done.append(ci)
 
     def send_far():
-        arrived(f2_t[0], g2far.at[0], at(h, y, x_mate))
-        for r in range(2):
-            arrived(f2_t[1 + r], g2far.at[1 + r], at(h, y, 2 * (1 - xp) + r))
-        zsend[...] = (hfar[0, xb] + g2far[0] + g2far[1] + g2far[2]).astype(BF16)
+        zsend[...] = collect(gfar[0, y, xb], gfar_in, gfar_t, (F1, F2)).astype(BF16)
         send(z_t, zsend, zrecv, z_mate)
 
     store_pgrad = pltpu.make_async_copy(pgrad, pgrad_hbm, load_sems.at[5])
     store_igrad = pltpu.make_async_copy(igrad, igrad_hbm, load_sems.at[6])
 
+    far_in()
     predict(N1)
-    far_columns()
+    send_teacher(jnp.logical_not(first_chunk))
+    predict(N2)
     sum_pair(N1)
-    send_teacher(jnp.logical_not(first_chunk))
-    turn(N1)
     predict(F1)
-    near_rows()
-    sum_quad(N1)
-    sum_pair(F1)
-    turn(F1)
-    residual(N1)
-    predict(F2)
-    sum_quad(F1)
-    sum_pair(F2)
-    turn(F2)
-    errors_pair(N1)
-    predict(N2)
-    residual(F1)
-    back(N1)
-    sum_quad(F2)
     sum_pair(N2)
     turn(N2)
-    grad(N1)
+    sum_pair(F1)
+    predict(F2)
+    sum_quad(N1)
+    sum_pair(F2)
+    sum_quad(F1)
+    sum_quad(F2)
+    turn(F1)
+    turn(F2)
+    residual(F1)
+    sum_quad(N2)
+    residual(F2)
     errors_pair(F1)
-    residual(F2)
-    sum_quad(N2)
+    residual(N1)
     back(F1)
-    second(N1)
+    errors_pair(F2)
     grad(F1)
-    errors_pair(F2)
     residual(N2)
     back(F2)
-    second(F1)
+    errors_pair(N1)
+    errors_pair(N2)
+    turn(N1)
+    back(N1)
+    grad(N1)
+    send_far()
+    back(N2)
     grad(F2)
-    errors_pair(N2)
-    second(F2)
-    back(N2)
-    send_far()
     grad(N2)
     store_pgrad.start()
     sent.extend(rows_out)
@@ -442,14 +407,9 @@
         op.wait_send()
     sent.clear()
 
-    arrived(n2_t[0], g2near, at(h, y_mate, x))
+    feature_grad = collect(gnear[0, yb, x], gnear_in, gnear_t, (N1, N2))
     arrived(z_t, zrecv, z_mate)
-    feature_grad = hnear[yb] + g2near[...].astype(F32) + zrecv[...].astype(F32)
-    for r in range(2):
-        for k in range(NX):
-            slot = NX * r + k
-            arrived(last_t[slot], g2last.at[slot], at(h, 2 * (1 - yp) + r, x_plus(NX - k)))
-            feature_grad = feature_grad + g2last[slot].astype(F32)
+    feature_grad = feature_grad + zrecv[...].astype(F32)
     upstream = feature_grad * sg_row
 
     inner = jnp.sum(upstream * unit, axis=1, keepdims=True)
@@ -504,13 +464,8 @@
             pltpu.VMEM((4, SECT) + piece, BF16),
             pltpu.VMEM((2, 2, NX, TOK, WS), BF16),
             pltpu.VMEM((2, NY, 2, TOK, WS), BF16),
-            pltpu.VMEM((3, 3, 2, TOK, WS), BF16),
-            pltpu.VMEM((2, TOK, WS), F32),
-            pltpu.VMEM((2, TOK, WS), BF16),
-            pltpu.VMEM((2, 2, TOK, WS), F32),
-            pltpu.VMEM((TOK, WS), BF16),
-            pltpu.VMEM((2 * NX, TOK, WS), BF16),
-            pltpu.VMEM((3, TOK, WS), F32),
+            pltpu.VMEM((15, TOK, WS), BF16),
+            pltpu.VMEM((15, TOK, WS), BF16),
             pltpu.VMEM((TOK, WS), BF16),
             pltpu.VMEM((TOK, WS), BF16),
             pltpu.SemaphoreType.DMA((7,)),

time: 106 us -> 100 us (0.943)
  the two profiles are of different devices: /device:TPU:6 before, /device:TPU:1 now
where the time goes in v3:
time: 100 us
  Pallas kernels  96.7 us (97%)
  other arithmetic  2.32 us (2%)
    pallas_call x1, Pallas kernels, body(): pl.pallas_call(kernel, out_shape=(jax.ShapeDtypeStruct((WS, WC), F32), ja...  96.7 us
    mul x1, other arithmetic, body(): return (summed * (1.0 / math.sqrt(TOKENS)), input_grad)  2.32 us

profile of v3, /device:TPU:1, one launch (start us, length us, event | category | flops | bytes accessed | tf_op | source)
XLA Modules:
  0.0 100.3 jit_solution(11794742900908917018)
XLA Ops:
  0.6 96.7 %shard_map.68 = (f32[512,512]{1,0:T(8,128)}, f32[32,512]{1,0:T(8,128)}) custom-call(bf16[32,1024]{1,0:T(8,128)(2,1)} %teacher_hbm.1, bf16[32,512]{1,0:T(8,128)(2,1)} %student_hbm.1, bf16[512,512]{1,0:T(8,128)(2,1)} %proj_hbm.1, f32[16,8,128]{2,1,0:T(8,128)} %bitcast.2, f32[16,4,128]{2,1,0:T(4,128)} %bitcast.3), custom_call_target="tpu_custom_call" | custom-call | tf_op jit(solution)/shard_map/pallas_call | solution.py:431
  97.3 0.0 copy-start
  97.3 2.3 %broadcast_multiply_fusion = f32[512,512]{1,0:T(8,128)} fusion(f32[512,512]{1,0:T(8,128)} %get-tuple-element.4), kind=kLoop, calls=%fused_computation | loop fusion | flops 262144 | bytes 2097152 | tf_op jit(solution)/shard_map/mul | solution.py:485
  99.6 0.0 copy-done
  99.6 0.6 copy.8
Async XLA Ops:
  97.3 2.3 %copy-start = (f32[32,512]{1,0:T(8,128)S(1)}, f32[32,512]{1,0:T(8,128)}, u32[]{:S(2)}) copy-start(f32[32,512]{1,0:T(8,128)} %get-tuple-element.9) | copy-start | bytes 196612

commit v4 on v3

--- a/solution.py
+++ b/solution.py
@@ -199,6 +199,8 @@
     pt[...] = proj[...].T
 
     total = finish_stat()
+    total_send[...] = total
+    send(total_t, total_send, total_far, z_mate)
     inv_s = lax.rsqrt(column(total, TOK) / DS + epsilon)
     unit = sf * inv_s
     feats[h, y, x] = (unit * sg_row).astype(BF16)
@@ -210,8 +212,6 @@
             send(base + here, feats.at[zh, y, x], feats.at[zh, y, x], at(h, *to), base + there)
 
     spread(N1)
-    total_send[...] = total
-    send(total_t, total_send, total_far, z_mate)
     spread(N2)
 
     inv_t = lax.rsqrt(column(total, 0) / DT + epsilon)
@@ -280,26 +280,26 @@
     def predict(ci):
         features_ready(ci)
         value = rows_of(ci)
-        for u in range(SECT):
-            half = jnp.dot(value, proj[:, u * HC : (u + 1) * HC], preferred_element_type=F32)
+        for theirs in (True, False):
+            u = 1 - c if theirs else c
+            half = jnp.dot(value, proj[:, pl.ds(pl.multiple_of(u * HC, HC), HC)], preferred_element_type=F32)
             part[ci, u] = half.reshape(2, 2, 2, TOK, HC)
-        send(pair_t[ci], part.at[ci, 1 - c], yrecv.at[ci], sibling)
+            if theirs:
+                send(pair_t[ci], part.at[ci, u], yrecv.at[ci], sibling)
 
     def sum_pair(ci):
         arrived(pair_t[ci], yrecv.at[ci], sibling)
-        value = part[ci, c] + yrecv[ci]
-        part[ci, c] = value
-        ssend[ci] = value.astype(BF16)
         for k in range(1, INQ):
             a, b = place(k)
+            ssend[ci, a, :, b] = (part[ci, c, a, :, b] + yrecv[ci, a, :, b]).astype(BF16)
             send(r1_t[ci][k - 1], ssend.at[ci, a, :, b], r1.at[ci, k - 1], in_quad(k))
+        acc[ci] = part[ci, c, pa, :, pb] + yrecv[ci, pa, :, pb]
 
     def sum_quad(ci):
+        value = acc[ci]
         for k in range(1, INQ):
             arrived(r1_t[ci][k - 1], r1.at[ci, k - 1], in_quad(INQ - k))
-        value = part[ci, c, pa, :, pb]
-        for k in range(INQ - 1):
-            value = value + r1[ci, k].astype(F32)
+            value = value + r1[ci, k - 1].astype(F32)
         acc[ci] = value
         arrived(tt[ci], trecv.at[ci], sibling)
         acc[ci, qd] = acc[ci, qd] - trecv[ci].astype(F32)
@@ -320,18 +320,20 @@
 
     def back(ci):
         arrived(es_t[ci], errs.at[ci, 1 - c], sibling)
-        value = None
-        for u in range(SECT):
-            term = jnp.dot(
-                errs[ci, u].reshape(CHUNK, HC), pt[u * HC : (u + 1) * HC, :], preferred_element_type=F32
-            )
-            value = term if value is None else value + term
-        value = value.astype(BF16)
         n = 0 if ci in (N1, F1) else 1
-        if ci in NEAR:
-            gnear[n] = value.reshape(2, NX, TOK, WS)
-        else:
-            gfar[n] = value.reshape(NY, 2, TOK, WS)
+        for half in range(2):
+            value = None
+            for u in range(SECT):
+                term = jnp.dot(
+                    errs[ci, u, half].reshape(CHUNK // 2, HC), pt[u * HC : (u + 1) * HC, :],
+                    preferred_element_type=F32,
+                )
+                value = term if value is None else value + term
+            value = value.astype(BF16)
+            if ci in NEAR:
+                gnear[n, half] = value.reshape(NX, TOK, WS)
+            else:
+                gfar[n, 2 * half : 2 * half + 2] = value.reshape(2, 2, TOK, WS)
         for to, _, there, here in peers(ci):
             if ci in NEAR:
                 send(gnear_t[here], gnear.at[n, to[0] % 2, to[1]], gnear_in.at[there], at(h, *to), gnear_t[0] + there)

time: 100 us -> 99.3 us (level)
  Pallas kernels: 96.7 us -> 95.5 us
    pallas_call x1, Pallas kernels: 96.7 us -> 95.5 us  [body(): pl.pallas_call(kernel, out_shape=(jax.ShapeDtypeStruct((WS, WC), F32), ja...]
where the time goes in v4:
time: 99.3 us; the launch traced here: 99.1 us
  Pallas kernels  95.5 us (96%)
  other arithmetic  2.32 us (2%)
    pallas_call x1, Pallas kernels, body(): pl.pallas_call(kernel, out_shape=(jax.ShapeDtypeStruct((WS, WC), F32), ja...  95.5 us
    mul x1, other arithmetic, body(): return (summed * (1.0 / math.sqrt(TOKENS)), input_grad)  2.32 us

profile of v4, /device:TPU:1, one launch (start us, length us, event | category | flops | bytes accessed | tf_op | source)
XLA Modules:
  0.0 99.1 jit_solution(2180671728553767113)
XLA Ops:
  0.6 95.5 %shard_map.68 = (f32[512,512]{1,0:T(8,128)}, f32[32,512]{1,0:T(8,128)}) custom-call(bf16[32,1024]{1,0:T(8,128)(2,1)} %teacher_hbm.1, bf16[32,512]{1,0:T(8,128)(2,1)} %student_hbm.1, bf16[512,512]{1,0:T(8,128)(2,1)} %proj_hbm.1, f32[16,8,128]{2,1,0:T(8,128)} %bitcast.2, f32[16,4,128]{2,1,0:T(4,128)} %bitcast.3), custom_call_target="tpu_custom_call" | custom-call | tf_op jit(solution)/shard_map/pallas_call | solution.py:433
  96.2 0.0 copy-start
  96.2 2.3 %broadcast_multiply_fusion = f32[512,512]{1,0:T(8,128)} fusion(f32[512,512]{1,0:T(8,128)} %get-tuple-element.4), kind=kLoop, calls=%fused_computation | loop fusion | flops 262144 | bytes 2097152 | tf_op jit(solution)/shard_map/mul | solution.py:487
  98.5 0.0 copy-done
  98.5 0.6 copy.8
Async XLA Ops:
  96.2 2.3 %copy-start = (f32[32,512]{1,0:T(8,128)S(1)}, f32[32,512]{1,0:T(8,128)}, u32[]{:S(2)}) copy-start(f32[32,512]{1,0:T(8,128)} %get-tuple-element.9) | copy-start | bytes 196612

commit v5 on v4

--- a/solution.py
+++ b/solution.py
@@ -30,6 +30,7 @@
 CHUNK = TENSOR * TOK
 LANES = 128
 SEMS = 144
+STORES = 8
 F32 = jnp.float32
 BF16 = jnp.bfloat16
 
@@ -357,7 +358,9 @@
         for u in range(SECT):
             term = jnp.dot(ft[ci], errs[ci, u].reshape(CHUNK, HC), preferred_element_type=F32)
             cols = slice(u * HC, (u + 1) * HC)
-            pgrad[:, cols] = term if not done else pgrad[:, cols] + term
+            if done:
+                term = pgrad[:, cols] + term
+            pgrad[:, cols] = term * (1.0 / math.sqrt(TOKENS)) if len(done) == 3 else term
         done.append(ci)
 
     def send_far():
@@ -427,10 +430,22 @@
     assert used[0] <= SEMS, used
 
 
+def store(pgrad_in, igrad_in, pgrad_out, igrad_out, sems):
+    step = WS // STORES
+    ops = [pltpu.make_async_copy(igrad_in, igrad_out, sems.at[STORES])]
+    for i in range(STORES):
+        rows = pl.ds(i * step, step)
+        ops.append(pltpu.make_async_copy(pgrad_in.at[rows], pgrad_out.at[rows], sems.at[i]))
+    for op in ops:
+        op.start()
+    for op in ops:
+        op.wait()
+
+
 def body(teacher_rows, student_rows, projector, teacher_gain, student_gain):
     anywhere = pl.BlockSpec(memory_space=pl.ANY)
     piece = (2, 2, 2, TOK, HC)
-    summed, input_grad = pl.pallas_call(
+    results = pl.pallas_call(
         kernel,
         out_shape=(
             jax.ShapeDtypeStruct((WS, WC), F32),
@@ -484,7 +499,17 @@
         teacher_gain.reshape(ST, WT // LANES, LANES),
         student_gain.reshape(ST, WS // LANES, LANES),
     )
-    return summed * (1.0 / math.sqrt(TOKENS)), input_grad
+    return pl.pallas_call(
+        store,
+        out_shape=(
+            jax.ShapeDtypeStruct((WS, WC), F32),
+            jax.ShapeDtypeStruct((TOK, WS), F32),
+        ),
+        in_specs=[anywhere] * 2,
+        out_specs=(anywhere, anywhere),
+        scratch_shapes=[pltpu.SemaphoreType.DMA((STORES + 1,))],
+        compiler_params=pltpu.CompilerParams(vmem_limit_bytes=60 * 1024 * 1024),
+    )(*results)
 
 
 def solution(mesh):

time: 99.3 us -> 131 us (1.32)
  Pallas kernels: 95.5 us -> 130 us
  other arithmetic: 2.32 us -> 0 us
    pallas_call x0 -> x1, Pallas kernels: none -> 34.9 us  [body(): pl.pallas_call(store, out_shape=(jax.ShapeDtypeStruct((WS, WC), F32), jax...]
    mul x1 -> x0, other arithmetic: 2.32 us -> none  [body(): return (summed * (1.0 / math.sqrt(TOKENS)), input_grad)]
where the time goes in v5:
time: 131 us
  Pallas kernels  130 us (99%)
    pallas_call x1, Pallas kernels, body(): pl.pallas_call(kernel, out_shape=(jax.ShapeDtypeStruct((WS, WC), F32), ja...  95.5 us
    pallas_call x1, Pallas kernels, body(): pl.pallas_call(store, out_shape=(jax.ShapeDtypeStruct((WS, WC), F32), jax...  34.9 us

profile of v5, /device:TPU:1, one launch (start us, length us, event | category | flops | bytes accessed | tf_op | source)
XLA Modules:
  0.0 131.1 jit_solution(8916986680959529333)
XLA Ops:
  0.6 95.5 %shard_map.68 = (f32[512,512]{1,0:T(8,128)}, f32[32,512]{1,0:T(8,128)}) custom-call(bf16[32,1024]{1,0:T(8,128)(2,1)} %teacher_hbm.1, bf16[32,512]{1,0:T(8,128)(2,1)} %student_hbm.1, bf16[512,512]{1,0:T(8,128)(2,1)} %proj_hbm.1, f32[16,8,128]{2,1,0:T(8,128)} %bitcast.2, f32[16,4,128]{2,1,0:T(4,128)} %bitcast.3), custom_call_target="tpu_custom_call" | custom-call | tf_op jit(solution)/shard_map/pallas_call | solution.py:448
  96.2 34.9 %shard_map.69 = (f32[512,512]{1,0:T(8,128)}, f32[32,512]{1,0:T(8,128)}) custom-call(f32[512,512]{1,0:T(8,128)} %get-tuple-element.4.pgrad_in, f32[32,512]{1,0:T(8,128)} %get-tuple-element.5.igrad_in), custom_call_target="tpu_custom_call" | custom-call | tf_op jit(solution)/shard_map/pallas_call | solution.py:502

commit v6 on v5

--- a/solution.py
+++ b/solution.py
@@ -30,7 +30,7 @@
 CHUNK = TENSOR * TOK
 LANES = 128
 SEMS = 144
-STORES = 8
+STORES = 4
 F32 = jnp.float32
 BF16 = jnp.bfloat16
 
@@ -430,15 +430,20 @@
     assert used[0] <= SEMS, used
 
 
-def store(pgrad_in, igrad_in, pgrad_out, igrad_out, sems):
+def store(pgrad_in, igrad_in, pgrad_out, igrad_out, pgrad, igrad, sems):
     step = WS // STORES
-    ops = [pltpu.make_async_copy(igrad_in, igrad_out, sems.at[STORES])]
+    hops = [(igrad_in, igrad, igrad_out)]
     for i in range(STORES):
         rows = pl.ds(i * step, step)
-        ops.append(pltpu.make_async_copy(pgrad_in.at[rows], pgrad_out.at[rows], sems.at[i]))
-    for op in ops:
+        hops.append((pgrad_in.at[rows], pgrad.at[rows], pgrad_out.at[rows]))
+    into = [pltpu.make_async_copy(a, b, sems.at[0, i]) for i, (a, b, _) in enumerate(hops)]
+    out = [pltpu.make_async_copy(b, c, sems.at[1, i]) for i, (_, b, c) in enumerate(hops)]
+    for op in into:
         op.start()
-    for op in ops:
+    for first, second in zip(into, out):
+        first.wait()
+        second.start()
+    for op in out:
         op.wait()
 
 
@@ -507,7 +512,11 @@
         ),
         in_specs=[anywhere] * 2,
         out_specs=(anywhere, anywhere),
-        scratch_shapes=[pltpu.SemaphoreType.DMA((STORES + 1,))],
+        scratch_shapes=[
+            pltpu.VMEM((WS, WC), F32),
+            pltpu.VMEM((TOK, WS), F32),
+            pltpu.SemaphoreType.DMA((2, STORES + 1)),
+        ],
         compiler_params=pltpu.CompilerParams(vmem_limit_bytes=60 * 1024 * 1024),
     )(*results)
 

time: 131 us -> 98.4 us (0.75)
  Pallas kernels: 130 us -> 97.6 us
    pallas_call x1, Pallas kernels: 34.9 us -> 2.04 us  [body(): pl.pallas_call(store, out_shape=(jax.ShapeDtypeStruct((WS, WC), F32), jax...]
where the time goes in v6:
time: 98.4 us; the launch traced here: 98.2 us
  Pallas kernels  97.6 us (99%)
    pallas_call x1, Pallas kernels, body(): pl.pallas_call(kernel, out_shape=(jax.ShapeDtypeStruct((WS, WC), F32), ja...  95.5 us
    pallas_call x1, Pallas kernels, body(): pl.pallas_call(store, out_shape=(jax.ShapeDtypeStruct((WS, WC), F32), jax...  2.04 us

profile of v6, /device:TPU:1, one launch (start us, length us, event | category | flops | bytes accessed | tf_op | source)
XLA Modules:
  0.0 98.2 jit_solution(17226519189451322000)
XLA Ops:
  0.6 95.5 %shard_map.68 = (f32[512,512]{1,0:T(8,128)}, f32[32,512]{1,0:T(8,128)}) custom-call(bf16[32,1024]{1,0:T(8,128)(2,1)} %teacher_hbm.1, bf16[32,512]{1,0:T(8,128)(2,1)} %student_hbm.1, bf16[512,512]{1,0:T(8,128)(2,1)} %proj_hbm.1, f32[16,8,128]{2,1,0:T(8,128)} %bitcast.2, f32[16,4,128]{2,1,0:T(4,128)} %bitcast.3), custom_call_target="tpu_custom_call" | custom-call | tf_op jit(solution)/shard_map/pallas_call | solution.py:453
  96.2 2.0 %shard_map.69 = (f32[512,512]{1,0:T(8,128)}, f32[32,512]{1,0:T(8,128)}) custom-call(f32[512,512]{1,0:T(8,128)} %get-tuple-element.4.pgrad_in, f32[32,512]{1,0:T(8,128)} %get-tuple-element.5.igrad_in), custom_call_target="tpu_custom_call" | custom-call | tf_op jit(solution)/shard_map/pallas_call | solution.py:507

commit v7 on v6

--- a/solution.py
+++ b/solution.py
@@ -42,7 +42,7 @@
     teacher_hbm, student_hbm, proj_hbm, tgain_hbm, sgain_hbm,
     pgrad_hbm, igrad_hbm,
     pgrad, igrad, pt, ft, teacher, student, proj, tgain, sgain,
-    stat, stat2, total_send, total_far, raw_far, feats, tsend, trecv, part, yrecv, ssend, r1, acc, a_send, r2,
+    stat, stat2, total_send, total_far, raw_far, feats, tsend, trecv, part, give, yrecv, ssend, r1, acc, a_send, r2,
     errs, gnear, gfar, gnear_in, gfar_in, zsend, zrecv,
     load_sems, send_sems, recv_sems,
 ):
@@ -284,17 +284,20 @@
         for theirs in (True, False):
             u = 1 - c if theirs else c
             half = jnp.dot(value, proj[:, pl.ds(pl.multiple_of(u * HC, HC), HC)], preferred_element_type=F32)
-            part[ci, u] = half.reshape(2, 2, 2, TOK, HC)
+            half = half.reshape(2, 2, 2, TOK, HC)
             if theirs:
-                send(pair_t[ci], part.at[ci, u], yrecv.at[ci], sibling)
+                give[ci] = half.astype(BF16)
+                send(pair_t[ci], give.at[ci], yrecv.at[ci], sibling)
+            else:
+                part[ci] = half
 
     def sum_pair(ci):
         arrived(pair_t[ci], yrecv.at[ci], sibling)
         for k in range(1, INQ):
             a, b = place(k)
-            ssend[ci, a, :, b] = (part[ci, c, a, :, b] + yrecv[ci, a, :, b]).astype(BF16)
+            ssend[ci, a, :, b] = (part[ci, a, :, b] + yrecv[ci, a, :, b].astype(F32)).astype(BF16)
             send(r1_t[ci][k - 1], ssend.at[ci, a, :, b], r1.at[ci, k - 1], in_quad(k))
-        acc[ci] = part[ci, c, pa, :, pb] + yrecv[ci, pa, :, pb]
+        acc[ci] = part[ci, pa, :, pb] + yrecv[ci, pa, :, pb].astype(F32)
 
     def sum_quad(ci):
         value = acc[ci]
@@ -374,6 +377,7 @@
     predict(N1)
     send_teacher(jnp.logical_not(first_chunk))
     predict(N2)
+    turn(N1)
     sum_pair(N1)
     predict(F1)
     sum_pair(N2)
@@ -398,20 +402,15 @@
     back(F2)
     errors_pair(N1)
     errors_pair(N2)
-    turn(N1)
     back(N1)
-    grad(N1)
     send_far()
     back(N2)
+    grad(N1)
     grad(F2)
     grad(N2)
     store_pgrad.start()
     sent.extend(rows_out)
 
-    for op in sent:
-        op.wait_send()
-    sent.clear()
-
     feature_grad = collect(gnear[0, yb, x], gnear_in, gnear_t, (N1, N2))
     arrived(z_t, zrecv, z_mate)
     feature_grad = feature_grad + zrecv[...].astype(F32)
@@ -419,12 +418,12 @@
 
     inner = jnp.sum(upstream * unit, axis=1, keepdims=True)
     stat2[st] = jnp.sum(jnp.where(lanes == rows, inner, zero), axis=0, keepdims=True)
-    inner_mean = column(exchange(stat2)(), 0) / DS
+    finish_stat2 = exchange(stat2)
+    for op in sent:
+        op.wait_send()
+    inner_mean = column(finish_stat2(), 0) / DS
     igrad[...] = inv_s * (upstream - unit * inner_mean)
     store_igrad.start()
-
-    for op in sent:
-        op.wait_send()
     store_pgrad.wait()
     store_igrad.wait()
     assert used[0] <= SEMS, used
@@ -476,8 +475,9 @@
             pltpu.VMEM((NZH, NY, NX, TOK, WS), BF16),
             pltpu.VMEM((2, SECT, TOK, HC), BF16),
             pltpu.VMEM((4, TOK, HC), BF16),
-            pltpu.VMEM((4, SECT) + piece, F32),
             pltpu.VMEM((4,) + piece, F32),
+            pltpu.VMEM((4,) + piece, BF16),
+            pltpu.VMEM((4,) + piece, BF16),
             pltpu.VMEM((4,) + piece, BF16),
             pltpu.VMEM((4, INQ - 1, QUADS, TOK, HC), BF16),
             pltpu.VMEM((4, QUADS, TOK, HC), F32),

time: 98.4 us -> 99.4 us (1.010)
  Pallas kernels: 97.6 us -> 98.6 us
    pallas_call x1, Pallas kernels: 95.5 us -> 96.6 us  [body(): pl.pallas_call(kernel, out_shape=(jax.ShapeDtypeStruct((WS, WC), F32), ja...]
where the time goes in v7:
time: 99.4 us; the launch traced here: 99.2 us
  Pallas kernels  98.6 us (99%)
    pallas_call x1, Pallas kernels, body(): pl.pallas_call(kernel, out_shape=(jax.ShapeDtypeStruct((WS, WC), F32), ja...  96.6 us
    pallas_call x1, Pallas kernels, body(): pl.pallas_call(store, out_shape=(jax.ShapeDtypeStruct((WS, WC), F32), jax...  2.04 us

profile of v7, /device:TPU:1, one launch (start us, length us, event | category | flops | bytes accessed | tf_op | source)
XLA Modules:
  0.0 99.2 jit_solution(4207609923094575356)
XLA Ops:
  0.6 96.6 %shard_map.68 = (f32[512,512]{1,0:T(8,128)}, f32[32,512]{1,0:T(8,128)}) custom-call(bf16[32,1024]{1,0:T(8,128)(2,1)} %teacher_hbm.1, bf16[32,512]{1,0:T(8,128)(2,1)} %student_hbm.1, bf16[512,512]{1,0:T(8,128)(2,1)} %proj_hbm.1, f32[16,8,128]{2,1,0:T(8,128)} %bitcast.2, f32[16,4,128]{2,1,0:T(4,128)} %bitcast.3), custom_call_target="tpu_custom_call" | custom-call | tf_op jit(solution)/shard_map/pallas_call | solution.py:452
  97.2 2.0 %shard_map.69 = (f32[512,512]{1,0:T(8,128)}, f32[32,512]{1,0:T(8,128)}) custom-call(f32[512,512]{1,0:T(8,128)} %get-tuple-element.4.pgrad_in, f32[32,512]{1,0:T(8,128)} %get-tuple-element.5.igrad_in), custom_call_target="tpu_custom_call" | custom-call | tf_op jit(solution)/shard_map/pallas_call | solution.py:507

commit v8 on v6

--- a/solution.py
+++ b/solution.py
@@ -186,9 +186,9 @@
 
         return finish
 
-    finish_stat = exchange(stat)
     raw_t, total_t = tickets(2)
     send(raw_t, student, raw_far, z_mate)
+    finish_stat = exchange(stat)
 
     loads[2].wait()
     sg = sgain[st]

time: 98.4 us -> 99 us (level)
  no operation moved by 1% of the time
where the time goes in v8:
time: 99 us; the launch traced here: 98.9 us
  Pallas kernels  98.2 us (99%)
    pallas_call x1, Pallas kernels, body(): pl.pallas_call(kernel, out_shape=(jax.ShapeDtypeStruct((WS, WC), F32), ja...  96.2 us
    pallas_call x1, Pallas kernels, body(): pl.pallas_call(store, out_shape=(jax.ShapeDtypeStruct((WS, WC), F32), jax...  2.04 us

profile of v8, /device:TPU:1, one launch (start us, length us, event | category | flops | bytes accessed | tf_op | source)
XLA Modules:
  0.0 98.9 jit_solution(1066978024876658876)
XLA Ops:
  0.6 96.2 %shard_map.68 = (f32[512,512]{1,0:T(8,128)}, f32[32,512]{1,0:T(8,128)}) custom-call(bf16[32,1024]{1,0:T(8,128)(2,1)} %teacher_hbm.1, bf16[32,512]{1,0:T(8,128)(2,1)} %student_hbm.1, bf16[512,512]{1,0:T(8,128)(2,1)} %proj_hbm.1, f32[16,8,128]{2,1,0:T(8,128)} %bitcast.2, f32[16,4,128]{2,1,0:T(4,128)} %bitcast.3), custom_call_target="tpu_custom_call" | custom-call | tf_op jit(solution)/shard_map/pallas_call | solution.py:453
  96.8 2.0 %shard_map.69 = (f32[512,512]{1,0:T(8,128)}, f32[32,512]{1,0:T(8,128)}) custom-call(f32[512,512]{1,0:T(8,128)} %get-tuple-element.4.pgrad_in, f32[32,512]{1,0:T(8,128)} %get-tuple-element.5.igrad_in), custom_call_target="tpu_custom_call" | custom-call | tf_op jit(solution)/shard_map/pallas_call | solution.py:507
